TPU v7x, 32 devices: a whole 2x2x4 slice. The times are simulated.
32 devices in a mesh: dp: 8 (over y, x, core), vocab: 4 (over z).
Axes of the slice: x: 2, y: 2, z: 4, core: 2. Of those that a mesh axis runs over, the one named last changes fastest.
Arguments:
- hidden_states: float32 [6144, 2048], P('dp'), may hold values from -8 to 8
- norm_gain: float32 [2048], replicated, may hold values from 0.5 to 1.5
- head_weight: bfloat16 [32768, 2048], P(('vocab', 'dp')), may hold values from -2 to 2
- target_ids: int32 [6144], P('dp'), may hold values from 0 to 32767
- lengths: int32 [8], P('dp'), may hold values from 1 to 768, as said below
Outputs:
- log_probs: float32 [6144], P('dp')
- entropies: float32 [6144], P('dp')
Inputs may be any that keep to these rules, and one draw needn't show every extreme that they name: `lengths`: live tokens of a sequence; some sequence fills all 768 slots.
All inputs are finite; a program needn't handle non-finite values.
Results may differ from a plain program's by a relative error of at most 0.0015.
Values may be sent and summed in bfloat16 or wider, within the bound.
A program may use at most 128 MiB of HBM per device.

v0:
```python
import jax
import jax.numpy as jnp
from jax import lax
from jax.sharding import PartitionSpec as P

epsilon = 1e-05
lowest = -1e30


def score_piece(normed, shard_piece):
    return lax.dot_general(
        normed, shard_piece, (((1,), (1,)), ((), ())), preferred_element_type=jnp.float32
    )


def update_stats(carry, logits, goal_cols):
    maxima, totals, tilted, target_logit = carry
    columns = jnp.arange(logits.shape[1], dtype=jnp.int32)
    highest = jnp.maximum(maxima, jnp.max(logits, axis=1))
    weights = jnp.exp(logits - highest[:, None])
    totals = jnp.sum(weights, axis=1)
    tilted = jnp.sum(weights * logits, axis=1)
    matched = jnp.where(columns[None, :] == goal_cols[:, None], logits, 0.0)
    target_logit = jnp.sum(matched, axis=1)
    return (highest, totals, tilted, target_logit)


def on_device(hidden_states, norm_gain, head_weight, target_ids, lengths):
    row_count = hidden_states.shape[0]
    scale = lax.rsqrt(jnp.mean(hidden_states * hidden_states, axis=1, keepdims=True) + epsilon)
    normed = (hidden_states * scale * norm_gain).astype(jnp.bfloat16)
    slice_width = head_weight.shape[0] * lax.axis_size("dp")
    goal_cols = target_ids - lax.axis_index("vocab") * slice_width
    live_count = lengths[0]
    positions = jnp.arange(row_count, dtype=jnp.int32)
    live_mask = positions < live_count
    initial = (
        jnp.full((row_count,), lowest, jnp.float32),
        jnp.zeros((row_count,), jnp.float32),
        jnp.zeros((row_count,), jnp.float32),
        jnp.zeros((row_count,), jnp.float32),
    )
    logits = score_piece(normed, lax.all_gather(head_weight, "dp", axis=0, tiled=True))
    stats = update_stats(initial, logits, goal_cols)
    maxima = lax.pmax(stats[0], "vocab")
    factor = jnp.exp(stats[0] - maxima)
    totals, tilted, target_logit = lax.psum(
        (stats[1] * factor, stats[2] * factor, stats[3]), "vocab"
    )
    log_total = maxima + jnp.log(totals)
    log_probs = jnp.where(live_mask, target_logit - log_total, 0.0)
    entropies = jnp.where(live_mask, log_total - tilted / totals, 0.0)
    return (log_probs, entropies)


def solution(mesh):
    in_specs = (P("dp", None), P(), P(("vocab", "dp"), None), P("dp"), P("dp"))
    out_specs = (P("dp"), P("dp"))
    return jax.shard_map(
        on_device, mesh=mesh, in_specs=in_specs, out_specs=out_specs, check_vma=False
    )
```

profile of v0, /device:TPU:0, one launch (start us, length us, event | category | flops | bytes accessed | tf_op | source)
XLA Modules:
  0.0 255.9 jit_solution(7895011486805984950)
XLA Ops:
  7.2 0.0 all-gather.2.cloned.1.call-start
  7.2 0.7 all-gather.2.cloned.1.call-update
  8.5 3.3 %multiply_reduce_fusion.1 = f32[768]{0:T(1024)S(1)} fusion(f32[768,2048]{1,0:T(8,128)} %param.5), kind=kLoop, calls=%fused_computation.6 | loop fusion | flops 3144960 | bytes 6294528 | tf_op jit(solution)/shard_map/reduce_sum | solution.py:30
  11.8 0.7 broadcast_subtract_fusion
  12.5 160.9 %all-gather.2.cloned.1.call-done = bf16[8192,2048]{1,0:T(8,128)(2,1)} async-done(((bf16[1024,2048]{1,0:T(8,128)(2,1)}), bf16[8192,2048]{1,0:T(8,128)(2,1)}) %all-gather.2.cloned.1.call-update) | async-done | bytes 33554448 | tf_op jit(solution)/shard_map/all_gather | solution.py:43
  173.4 34.8 %fusion.6 = (f32[768]{0:T(1024)S(1)}, f32[768,8192]{1,0:T(8,128)}) fusion(bf16[8192,2048]{1,0:T(8,128)(2,1)} %all-gather.2.cloned.1.call-done, f32[768,2048]{1,0:T(8,128)} %param.5, f32[2048]{0:T(1024)} %param.6, f32[768]{0:T(1024)S(1)} %add_rsqrt_fusion), kind=kOutput, calls=%fused_computation.20 | convolution fusion | flops 25780813824 | bytes 65026048 | tf_op jit(solution)/shard_map/dot_general | solution.py:11
  208.2 11.7 %pmax.7 = f32[768]{0:T(1024)S(1)} all-reduce(f32[768]{0:T(1024)S(1)} %broadcast_maximum_fusion), channel_id=1, replica_groups=mesh['dp'=8,'vocab'=4] {'vocab'}, use_global_device_ids=true, to_apply=%region_4.5 | all-reduce | flops 768 | bytes 6144 | tf_op jit(solution)/shard_map/pmax | solution.py:45
  219.9 13.1 %multiply_reduce_fusion = (f32[768]{0:T(1024)S(1)}, f32[768]{0:T(1024)S(1)}, f32[768]{0:T(1024)S(1)}) fusion(f32[768,8192]{1,0:T(8,128)} %get-tuple-element.13, f32[768]{0:T(1024)S(1)} %broadcast_maximum_fusion, s32[768]{0:T(1024)S(1)} %broadcast_subtract_fusion), kind=kLoop, calls=%fused_computation | loop fusion | flops 44037888 | bytes 25181184 | tf_op jit(solution)/shard_map/reduce_sum | solution.py:22
  233.0 15.5 %all-reduce = (f32[768]{0:T(1024)S(1)}, f32[768]{0:T(1024)S(1)}, f32[768]{0:T(1024)S(1)}) all-reduce(f32[768]{0:T(1024)S(1)} %get-tuple-element.4, f32[768]{0:T(1024)S(1)} %get-tuple-element.11, f32[768]{0:T(1024)S(1)} %get-tuple-element.10), channel_id=1, replica_groups=mesh['dp'=8,'vocab'=4] {'vocab'}, use_global_device_ids=true, to_apply=%region_2.0 | all-reduce | flops 2304 | bytes 18432 | tf_op jit(solution)/shard_map/psum | solution.py:47
  248.5 0.6 subtract_select_fusion
  (3 shorter events, 0.0 us)
Async XLA Ops:
  7.2 166.2 %all-gather.2.cloned.1.call-start = ((), (), s32[]{:S(2)}) async-start(), calls=%async_computation | async-start | bytes 37748736 | tf_op jit(solution)/shard_map/all_gather | solution.py:43
Sparse Core Ops, SparseCore 0:
  9.9 163.4 all-gather.1
where the time goes:
time: 256 us
  waiting for transfers between devices  162 us (63%)
  matrix products  34.8 us (14%)
  blocking collectives  27.2 us (11%)
  other arithmetic  17.7 us (7%)
  between operations  14.7 us (6%)
    all_gather x1, waiting for transfers between devices, on_device(): lax.all_gather(head_weight, 'dp', axis=0, tiled=True)  161 us
    dot_general x1, matrix products, score_piece(): lax.dot_general(normed, shard_piece, (((1,), (1,)), ((), ())), preferred_...  34.8 us
    psum x1, blocking collectives, on_device(): lax.psum((stats[1] * factor, stats[2] * factor, stats[3]), 'vocab')  15.5 us
    reduce_sum x1, other arithmetic, update_stats(): tilted = jnp.sum(weights * logits, axis=1)  13.1 us
    pmax x1, blocking collectives, on_device(): maxima = lax.pmax(stats[0], 'vocab')  11.7 us
  transfers between devices with their start and end apart: 1, of which 1 were waited for; matrix products, arithmetic and copies ran while one was open for 2% of the time, Pallas kernels for 0%

commit v1 on v0

v1 whole, which is shorter than its diff:
```python
import functools

import jax
import jax.numpy as jnp
from jax import lax
from jax.experimental import pallas as pl
from jax.experimental.pallas import tpu as pltpu
from jax.sharding import PartitionSpec as P

epsilon = 1e-05
lowest = -1e30
MESH = pl.DeviceIdType.MESH
BLOCK = 512


def merge(parts):
    top = parts[0][:, 0:1, :]
    for part in parts[1:]:
        top = jnp.maximum(top, part[:, 0:1, :])
    total = tilted = target = jnp.zeros_like(top)
    for part in parts:
        factor = jnp.exp(part[:, 0:1, :] - top)
        total = total + part[:, 1:2, :] * factor
        tilted = tilted + part[:, 2:3, :] * factor
        target = target + part[:, 3:4, :]
    return top, total, tilted, target


def rows_of(values, shape):
    axis = len(shape) - 2
    row = lax.broadcasted_iota(jnp.int32, shape, axis)
    tile = jnp.zeros(shape, jnp.float32)
    for i, value in enumerate(values):
        tile = jnp.where(row == i, value, tile)
    return tile


def kernel(nz, hid, gain, head, goal, out, T, W, raw, tgt, st, rs, rz,
           hid_sem, w_sem, xs, xr, ys, yr, zs, zr, gs, gr, ss, sr, vs, vr):
    dp = lax.axis_index("dp")
    z = lax.axis_index("vocab")
    core = lax.rem(dp, 2)
    xc = lax.rem(lax.div(dp, 2), 2)
    yc = lax.div(dp, 4)
    p = lax.rem(z, 2)
    q = p + 1
    s = 2 * p
    m = 2 - s
    near_core = (dp + 1 - 2 * core, z)
    near_x = (dp + 2 - 4 * xc, z)
    near_y = (dp + 4 - 8 * yc, z)
    near_d = (dp + 2 - 4 * xc + 4 - 8 * yc, z)
    near_z = (dp, z + 1 - 2 * p)
    far_z = [(dp, lax.rem(z + k, nz)) for k in range(1, nz)]
    partners = [near_core, near_x, near_y, near_d] + far_z

    third = T.shape[2]
    half = third // 2
    entries = head.shape[0]
    base = (z * lax.axis_size("dp") + dp - core) * entries

    def load(t):
        return pltpu.make_async_copy(
            hid.at[pl.ds(t * third, third)], raw.at[t], hid_sem.at[t]
        )

    def send(src, dst, send_sem, recv_sem, where):
        return pltpu.make_async_remote_copy(
            src_ref=src, dst_ref=dst, send_sem=send_sem, recv_sem=recv_sem,
            device_id=where, device_id_type=MESH,
        )

    def piece(slot, t, k):
        return T.at[slot, t, pl.ds((k % 2) * half, half)]

    def X(k):
        if k < 4:
            t = q if k < 2 else p
            return send(piece(0, t, k), piece(1, t, k), xs.at[k], xr.at[k], near_x)
        return send(piece(2, p, k), piece(3, p, k), xs.at[k], xr.at[k], near_x)

    def Y(k):
        if k < 4:
            t = p if k < 2 else q
            return send(piece(0, t, k), piece(2, t, k), ys.at[k], yr.at[k], near_y)
        return send(piece(1, q, k), piece(3, q, k), ys.at[k], yr.at[k], near_y)

    def Z(k):
        slot = (2 - p, 1 + p, 3)[k // 2]
        return send(piece(slot, s, k), piece(slot, s, k), zs.at[k], zr.at[k], near_z)

    def Z_in(k):
        slot = (1 + p, 2 - p, 3)[k // 2]
        return send(piece(slot, m, k), piece(slot, m, k), zs.at[k], zr.at[k], near_z)

    own_rows = pl.ds(core * entries, entries)
    other_rows = pl.ds((1 - core) * entries, entries)
    w_local = pltpu.make_async_copy(head, W.at[own_rows], w_sem.at[0])
    w_send = send(head, W.at[own_rows], w_sem.at[1], w_sem.at[2], near_core)
    w_in = send(head, W.at[other_rows], w_sem.at[1], w_sem.at[2], near_core)
    goals = [
        send(goal, tgt.at[j], gs.at[j - 1], gr.at[j - 1], where)
        for j, where in ((1, near_x), (2, near_y), (3, near_d))
    ]
    stats = [
        send(st.at[j], rs.at[j], ss.at[j - 1], sr.at[j - 1], where)
        for j, where in ((1, near_x), (2, near_y), (3, near_d))
    ]

    for t in (p, q, m):
        load(t).start()
    barrier = pltpu.get_barrier_semaphore()
    for where in partners:
        pl.semaphore_signal(barrier, inc=1, device_id=where, device_id_type=MESH)
    w_local.start()

    def normalise(t):
        load(t).wait()
        states = raw[t]
        scale = lax.rsqrt(jnp.mean(states * states, axis=1, keepdims=True) + epsilon)
        T[0, t] = (states * scale * gain[...]).astype(jnp.bfloat16)

    normalise(p)
    pl.semaphore_wait(barrier, len(partners))
    Y(0).start()
    w_send.start()
    Y(1).start()
    normalise(q)
    X(0).start()
    X(1).start()
    for copy in goals:
        copy.start()
    normalise(m)
    tgt[0] = goal[...]

    def unit(slot, t):
        wanted = tgt[slot, t, 0:1, :] - base

        def body(i, carry):
            top, total, tilted, target = carry
            rows = pl.ds(pl.multiple_of(i * BLOCK, BLOCK), BLOCK)
            logits = lax.dot_general(
                W[rows, :], T[slot, t], (((1,), (1,)), ((), ())),
                preferred_element_type=jnp.float32,
            )
            entry = lax.broadcasted_iota(jnp.int32, logits.shape, 0)
            hit = jnp.where(entry == wanted - i * BLOCK, logits, 0.0)
            target = target + jnp.sum(hit.reshape(BLOCK // 8, 8, third), axis=0)
            logits = logits.reshape(BLOCK // 8, 8, third)
            higher = jnp.maximum(top, jnp.max(logits, axis=0))
            factor = jnp.exp(top - higher)
            weights = jnp.exp(logits - higher[None])
            total = total * factor + jnp.sum(weights, axis=0)
            tilted = tilted * factor + jnp.sum(weights * logits, axis=0)
            return higher, total, tilted, target

        zero = jnp.zeros((8, third), jnp.float32)
        top, total, tilted, target = lax.fori_loop(
            0, W.shape[0] // BLOCK, body, (jnp.full((8, third), lowest, jnp.float32), zero, zero, zero)
        )
        highest = jnp.max(top, axis=0, keepdims=True)
        factor = jnp.exp(top - highest)
        st[slot, t] = rows_of(
            (
                highest,
                jnp.sum(total * factor, axis=0, keepdims=True),
                jnp.sum(tilted * factor, axis=0, keepdims=True),
                jnp.sum(target, axis=0, keepdims=True),
            ),
            (8, third),
        )

    def wave(k):
        X(k).wait_recv()
        Y(k).wait_recv()
        if k < 4:
            X(k + 2).start()
            Y(k + 2).start()
        Z(k).start()

    def units(count, pick):
        def step(u, carry):
            unit(*pick(u))
            return carry

        lax.fori_loop(0, count, step, 0)

    w_local.wait()
    w_in.wait_recv()
    units(2, lambda u: (0, p + u))
    wave(0)
    units(1, lambda u: (0, m))
    for copy in goals:
        copy.wait_recv()
    wave(1)
    units(2, lambda u: (1 + u, q - u))
    wave(2)
    Z_in(0).wait_recv()
    Z_in(1).wait_recv()
    wave(3)
    units(3, lambda u: (jnp.where(u == 2, 1 + p, 1 + u), jnp.where(u == 2, m, p + u)))
    wave(4)
    Z_in(2).wait_recv()
    Z_in(3).wait_recv()
    units(1, lambda u: (2 - p, m))
    stats[0].start()
    stats[1].start()
    wave(5)
    units(2, lambda u: (3, p + u))
    Z_in(4).wait_recv()
    Z_in(5).wait_recv()
    units(1, lambda u: (3, m))
    stats[2].start()
    for copy in stats:
        copy.wait_recv()
    top, total, tilted, target = merge([st[0], rs[1], rs[2], rs[3]])
    rz[z] = rows_of((top, total, tilted, target), (3, 8, third))

    def V(k, source):
        return send(rz.at[source], rz.at[source], vs.at[k - 1], vr.at[k - 1], far_z[k - 1])

    for k in range(1, nz):
        V(k, z).start()
    for k in range(1, nz):
        V(k, lax.rem(z + nz - k, nz)).wait_recv()
    top, total, tilted, target = merge([rz[i] for i in range(nz)])
    log_total = top + jnp.log(total)
    out[...] = rows_of((target - log_total, log_total - tilted / total), (3, 8, third))

    w_send.wait_send()
    for k in range(6):
        X(k).wait_send()
        Y(k).wait_send()
        Z(k).wait_send()
    for copy in goals + stats:
        copy.wait_send()
    for k in range(1, nz):
        V(k, z).wait_send()


def fused(nz, hidden_states, norm_gain, head_weight, target_ids, lengths):
    rows, width = hidden_states.shape
    entries = head_weight.shape[0]
    third = rows // 3
    goal = jnp.broadcast_to(target_ids.reshape(3, 1, third), (3, 8, third))
    dma = pltpu.SemaphoreType.DMA
    any_space = pl.BlockSpec(memory_space=pl.ANY)
    vmem = pl.BlockSpec(memory_space=pltpu.VMEM)
    scores = pl.pallas_call(
        functools.partial(kernel, nz),
        out_shape=jax.ShapeDtypeStruct((3, 8, third), jnp.float32),
        in_specs=[any_space, vmem, any_space, vmem],
        out_specs=vmem,
        scratch_shapes=[
            pltpu.VMEM((4, 3, third, width), jnp.bfloat16),
            pltpu.VMEM((2 * entries, width), jnp.bfloat16),
            pltpu.VMEM((3, third, width), jnp.float32),
            pltpu.VMEM((4, 3, 8, third), jnp.int32),
            pltpu.VMEM((4, 3, 8, third), jnp.float32),
            pltpu.VMEM((4, 3, 8, third), jnp.float32),
            pltpu.VMEM((nz, 3, 8, third), jnp.float32),
            dma((3,)), dma((3,)),
            dma((6,)), dma((6,)), dma((6,)), dma((6,)), dma((6,)), dma((6,)),
            dma((3,)), dma((3,)), dma((3,)), dma((3,)),
            dma((nz - 1,)), dma((nz - 1,)),
        ],
        compiler_params=pltpu.CompilerParams(
            collective_id=0, has_side_effects=True, vmem_limit_bytes=56 * 1024 * 1024
        ),
        cost_estimate=pl.CostEstimate(
            flops=2 * 4 * rows * 2 * entries * width,
            bytes_accessed=rows * width * 4 + entries * width * 2,
            transcendentals=4 * rows * 2 * entries,
        ),
    )(hidden_states, norm_gain.reshape(1, width), head_weight, goal)
    live = jnp.arange(rows, dtype=jnp.int32) < lengths[0]
    log_probs = jnp.where(live, scores[:, 0, :].reshape(rows), 0.0)
    entropies = jnp.where(live, scores[:, 1, :].reshape(rows), 0.0)
    return (log_probs, entropies)


def gathered(hidden_states, norm_gain, head_weight, target_ids, lengths):
    row_count = hidden_states.shape[0]
    scale = lax.rsqrt(jnp.mean(hidden_states * hidden_states, axis=1, keepdims=True) + epsilon)
    normed = (hidden_states * scale * norm_gain).astype(jnp.bfloat16)
    slice_width = head_weight.shape[0] * lax.axis_size("dp")
    goal_cols = target_ids - lax.axis_index("vocab") * slice_width
    live_mask = jnp.arange(row_count, dtype=jnp.int32) < lengths[0]
    logits = lax.dot_general(
        normed, lax.all_gather(head_weight, "dp", axis=0, tiled=True),
        (((1,), (1,)), ((), ())), preferred_element_type=jnp.float32,
    )
    columns = jnp.arange(logits.shape[1], dtype=jnp.int32)
    highest = jnp.max(logits, axis=1)
    weights = jnp.exp(logits - highest[:, None])
    matched = jnp.where(columns[None, :] == goal_cols[:, None], logits, 0.0)
    maxima = lax.pmax(highest, "vocab")
    factor = jnp.exp(highest - maxima)
    totals, tilted, target_logit = lax.psum(
        (
            jnp.sum(weights, axis=1) * factor,
            jnp.sum(weights * logits, axis=1) * factor,
            jnp.sum(matched, axis=1),
        ),
        "vocab",
    )
    log_total = maxima + jnp.log(totals)
    log_probs = jnp.where(live_mask, target_logit - log_total, 0.0)
    entropies = jnp.where(live_mask, log_total - tilted / totals, 0.0)
    return (log_probs, entropies)


def solution(mesh):
    ndp, nz = mesh.shape["dp"], mesh.shape["vocab"]

    def on_device(*args):
        rows, width = args[0].shape
        entries = args[2].shape[0]
        fits = (
            ndp == 8 and nz % 2 == 0 and rows % 768 == 0 and width % 128 == 0
            and 2 * entries % BLOCK == 0
            and 20 * rows * width + 4 * entries * width < 40 * 1024 * 1024
        )
        return fused(nz, *args) if fits else gathered(*args)

    in_specs = (P("dp", None), P(), P(("vocab", "dp"), None), P("dp"), P("dp"))
    out_specs = (P("dp"), P("dp"))
    return jax.shard_map(
        on_device, mesh=mesh, in_specs=in_specs, out_specs=out_specs, check_vma=False
    )
```

time: 256 us -> 107 us (0.42)
  waiting for transfers between devices: 162 us -> 0 us
  Pallas kernels: 0 us -> 102 us
  matrix products: 34.8 us -> 0 us
  blocking collectives: 27.2 us -> 0 us
  other arithmetic: 17.7 us -> 0.6 us
  between operations: 14.7 us -> 1.29 us
    all_gather x1 -> x0, waiting for transfers between devices: 161 us -> none  [on_device(): lax.all_gather(head_weight, 'dp', axis=0, tiled=True)]
    pallas_call x0 -> x1, Pallas kernels: none -> 102 us  [fused(): pl.pallas_call(functools.partial(kernel, nz), out_shape=jax.ShapeDtypeStr...]
    dot_general x1 -> x0, matrix products: 34.8 us -> none  [score_piece(): lax.dot_general(normed, shard_piece, (((1,), (1,)), ((), ())), preferred_...]
    reduce_sum x2 -> x0, other arithmetic: 16.3 us -> none  [the longest x1 13.1 us: update_stats(): tilted = jnp.sum(weights * logits, axis=1)]
    psum x1 -> x0, blocking collectives: 15.5 us -> none  [on_device(): lax.psum((stats[1] * factor, stats[2] * factor, stats[3]), 'vocab')]
    pmax x1 -> x0, blocking collectives: 11.7 us -> none  [on_device(): maxima = lax.pmax(stats[0], 'vocab')]
  transfers between devices with their start and end apart: 1 -> 0, of which waited for: 1 -> 0; matrix products, arithmetic and copies ran while one was open for 2% -> 0% of each run, Pallas kernels for 0% -> 0%
where the time goes in v1:
time: 107 us; the launch traced here: 106 us
  Pallas kernels  102 us (95%)
  local copies, waits for them, and re-layouts  2.15 us (2%)
  between operations  1.29 us (1%)
    pallas_call x1, Pallas kernels, fused(): pl.pallas_call(functools.partial(kernel, nz), out_shape=jax.ShapeDtypeStr...  102 us

profile of v1, /device:TPU:0, one launch (start us, length us, event | category | flops | bytes accessed | tf_op | source)
XLA Modules:
  0.0 106.5 jit_solution(13934753185551204975)
XLA Ops:
  0.6 0.7 broadcast_in_dim.12
  1.3 0.6 broadcast_in_dim.13.goal
  1.9 102.4 %shard_map.68 = f32[3,8,256]{2,1,0:T(8,128)} custom-call(f32[768,2048]{1,0:T(8,128)} %hid.1, f32[1,2048]{1,0:T(1,128)} %bitcast.3, bf16[1024,2048]{1,0:T(8,128)(2,1)} %head.1, s32[3,8,256]{2,1,0:T(8,128)} %broadcast_in_dim.13.goal), custom_call_target="tpu_custom_call" | custom-call | flops 25769803776 | bytes 10485760 | tf_op jit(solution)/shard_map/pallas_call | solution.py:249
  104.4 0.8 slice_reduce_fusion
  105.9 0.6 fusion
  (2 shorter events, 0.0 us)

commit v2 on v1

--- a/solution.py
+++ b/solution.py
@@ -11,6 +11,8 @@
 lowest = -1e30
 MESH = pl.DeviceIdType.MESH
 BLOCK = 512
+PIECES = 4
+WINDOW = 2
 
 
 def merge(parts):
@@ -35,7 +37,7 @@
     return tile
 
 
-def kernel(nz, hid, gain, head, goal, out, T, W, raw, tgt, st, rs, rz,
+def kernel(nz, hid, gain, head, goal, out, T, W, raw, tgt, acc, st, rs, rz,
            hid_sem, w_sem, xs, xr, ys, yr, zs, zr, gs, gr, ss, sr, vs, vr):
     dp = lax.axis_index("dp")
     z = lax.axis_index("vocab")
@@ -55,7 +57,8 @@
     partners = [near_core, near_x, near_y, near_d] + far_z
 
     third = T.shape[2]
-    half = third // 2
+    size = third // PIECES
+    waves = 3 * PIECES
     entries = head.shape[0]
     base = (z * lax.axis_size("dp") + dp - core) * entries
 
@@ -71,26 +74,26 @@
         )
 
     def piece(slot, t, k):
-        return T.at[slot, t, pl.ds((k % 2) * half, half)]
+        return T.at[slot, t, pl.ds(lax.rem(k, PIECES) * size, size)]
 
     def X(k):
-        if k < 4:
-            t = q if k < 2 else p
-            return send(piece(0, t, k), piece(1, t, k), xs.at[k], xr.at[k], near_x)
-        return send(piece(2, p, k), piece(3, p, k), xs.at[k], xr.at[k], near_x)
+        g = lax.div(k, PIECES)
+        d, t = lax.div(g, 2), q - lax.div(g + 1, 2)
+        return send(piece(2 * d, t, k), piece(1 + 2 * d, t, k), xs.at[k], xr.at[k], near_x)
 
     def Y(k):
-        if k < 4:
-            t = p if k < 2 else q
-            return send(piece(0, t, k), piece(2, t, k), ys.at[k], yr.at[k], near_y)
-        return send(piece(1, q, k), piece(3, q, k), ys.at[k], yr.at[k], near_y)
+        g = lax.div(k, PIECES)
+        d, t = lax.div(g, 2), p + lax.div(g + 1, 2)
+        return send(piece(d, t, k), piece(2 + d, t, k), ys.at[k], yr.at[k], near_y)
 
     def Z(k):
-        slot = (2 - p, 1 + p, 3)[k // 2]
+        g = lax.div(k, PIECES)
+        slot = jnp.where(g == 0, 2 - p, jnp.where(g == 1, 1 + p, 3))
         return send(piece(slot, s, k), piece(slot, s, k), zs.at[k], zr.at[k], near_z)
 
     def Z_in(k):
-        slot = (1 + p, 2 - p, 3)[k // 2]
+        g = lax.div(k, PIECES)
+        slot = jnp.where(g == 0, 1 + p, jnp.where(g == 1, 2 - p, 3))
         return send(piece(slot, m, k), piece(slot, m, k), zs.at[k], zr.at[k], near_z)
 
     own_rows = pl.ds(core * entries, entries)
@@ -122,94 +125,118 @@
 
     normalise(p)
     pl.semaphore_wait(barrier, len(partners))
-    Y(0).start()
+    for k in range(WINDOW):
+        Y(k).start()
     w_send.start()
-    Y(1).start()
     normalise(q)
-    X(0).start()
-    X(1).start()
+    for k in range(WINDOW):
+        X(k).start()
     for copy in goals:
         copy.start()
     normalise(m)
     tgt[0] = goal[...]
-
-    def unit(slot, t):
+    row = lax.broadcasted_iota(jnp.int32, acc.shape, 2)
+    acc[...] = jnp.where(row == 0, lowest, 0.0)
+    w_local.wait()
+    w_in.wait_recv()
+
+    def block(slot, t, i):
         wanted = tgt[slot, t, 0:1, :] - base
-
-        def body(i, carry):
-            top, total, tilted, target = carry
-            rows = pl.ds(pl.multiple_of(i * BLOCK, BLOCK), BLOCK)
-            logits = lax.dot_general(
-                W[rows, :], T[slot, t], (((1,), (1,)), ((), ())),
-                preferred_element_type=jnp.float32,
+        rows = pl.ds(pl.multiple_of(i * BLOCK, BLOCK), BLOCK)
+        logits = lax.dot_general(
+            W[rows, :], T[slot, t], (((1,), (1,)), ((), ())),
+            preferred_element_type=jnp.float32,
+        )
+        entry = lax.broadcasted_iota(jnp.int32, logits.shape, 0)
+        hit = jnp.where(entry == wanted - i * BLOCK, logits, 0.0)
+        logits = logits.reshape(BLOCK // 8, 8, third)
+        top = acc[slot, t, 0]
+        higher = jnp.maximum(top, jnp.max(logits, axis=0))
+        factor = jnp.exp(top - higher)
+        weights = jnp.exp(logits - higher[None])
+        acc[slot, t, 0] = higher
+        acc[slot, t, 1] = acc[slot, t, 1] * factor + jnp.sum(weights, axis=0)
+        acc[slot, t, 2] = acc[slot, t, 2] * factor + jnp.sum(weights * logits, axis=0)
+        acc[slot, t, 3] = acc[slot, t, 3] + jnp.sum(hit.reshape(BLOCK // 8, 8, third), axis=0)
+
+    blocks = W.shape[0] // BLOCK
+
+    def pick(g, u):
+        if g == 0:
+            return 0, jnp.where(u == 2, m, p + u)
+        if g == 1:
+            return jnp.where(u == 2, 1 + p, 1 + u), jnp.where(u == 2, m, q - u)
+        if g == 2:
+            return jnp.where(u == 2, 2 - p, 1 + u), jnp.where(u == 2, m, p + u)
+        return 3, jnp.where(u == 2, m, p + u)
+
+    def work(g, first, count):
+        def step(b, carry):
+            slot, t = pick(g, lax.div(b, blocks))
+            block(slot, t, lax.rem(b, blocks))
+            return carry
+
+        lax.fori_loop(first, first + count, step, 0)
+
+    def arrive(g):
+        def step(j, carry):
+            Z_in(g * PIECES + j).wait_recv()
+            return carry
+
+        lax.fori_loop(0, PIECES, step, 0)
+
+    def finish(slot):
+        for t in range(3):
+            top = acc[slot, t, 0]
+            highest = jnp.max(top, axis=0, keepdims=True)
+            factor = jnp.exp(top - highest)
+            st[slot, t] = rows_of(
+                (
+                    highest,
+                    jnp.sum(acc[slot, t, 1] * factor, axis=0, keepdims=True),
+                    jnp.sum(acc[slot, t, 2] * factor, axis=0, keepdims=True),
+                    jnp.sum(acc[slot, t, 3], axis=0, keepdims=True),
+                ),
+                (8, third),
             )
-            entry = lax.broadcasted_iota(jnp.int32, logits.shape, 0)
-            hit = jnp.where(entry == wanted - i * BLOCK, logits, 0.0)
-            target = target + jnp.sum(hit.reshape(BLOCK // 8, 8, third), axis=0)
-            logits = logits.reshape(BLOCK // 8, 8, third)
-            higher = jnp.maximum(top, jnp.max(logits, axis=0))
-            factor = jnp.exp(top - higher)
-            weights = jnp.exp(logits - higher[None])
-            total = total * factor + jnp.sum(weights, axis=0)
-            tilted = tilted * factor + jnp.sum(weights * logits, axis=0)
-            return higher, total, tilted, target
-
-        zero = jnp.zeros((8, third), jnp.float32)
-        top, total, tilted, target = lax.fori_loop(
-            0, W.shape[0] // BLOCK, body, (jnp.full((8, third), lowest, jnp.float32), zero, zero, zero)
-        )
-        highest = jnp.max(top, axis=0, keepdims=True)
-        factor = jnp.exp(top - highest)
-        st[slot, t] = rows_of(
-            (
-                highest,
-                jnp.sum(total * factor, axis=0, keepdims=True),
-                jnp.sum(tilted * factor, axis=0, keepdims=True),
-                jnp.sum(target, axis=0, keepdims=True),
-            ),
-            (8, third),
-        )
-
-    def wave(k):
+
+    def wave(k, more):
         X(k).wait_recv()
         Y(k).wait_recv()
-        if k < 4:
-            X(k + 2).start()
-            Y(k + 2).start()
+        if more:
+            X(k + WINDOW).start()
+            Y(k + WINDOW).start()
         Z(k).start()
 
-    def units(count, pick):
-        def step(u, carry):
-            unit(*pick(u))
+    share = 3 * blocks // PIECES
+
+    def phase(g, first, last, more):
+        def step(j, carry):
+            wave(g * PIECES + j, more)
+            work(g, j * share, share)
             return carry
 
-        lax.fori_loop(0, count, step, 0)
-
-    w_local.wait()
-    w_in.wait_recv()
-    units(2, lambda u: (0, p + u))
-    wave(0)
-    units(1, lambda u: (0, m))
+        lax.fori_loop(first, last, step, 0)
+
+    ready = PIECES // 2
+    phase(0, 0, PIECES, True)
     for copy in goals:
         copy.wait_recv()
-    wave(1)
-    units(2, lambda u: (1 + u, q - u))
-    wave(2)
-    Z_in(0).wait_recv()
-    Z_in(1).wait_recv()
-    wave(3)
-    units(3, lambda u: (jnp.where(u == 2, 1 + p, 1 + u), jnp.where(u == 2, m, p + u)))
-    wave(4)
-    Z_in(2).wait_recv()
-    Z_in(3).wait_recv()
-    units(1, lambda u: (2 - p, m))
+    phase(1, 0, ready, True)
+    arrive(0)
+    phase(1, ready, PIECES, True)
+    phase(2, 0, ready, True)
+    arrive(1)
+    phase(2, ready, PIECES, False)
+    finish(1)
+    finish(2)
     stats[0].start()
     stats[1].start()
-    wave(5)
-    units(2, lambda u: (3, p + u))
-    Z_in(4).wait_recv()
-    Z_in(5).wait_recv()
-    units(1, lambda u: (3, m))
+    work(3, 0, 2 * blocks)
+    finish(0)
+    arrive(2)
+    work(3, 2 * blocks, blocks)
+    finish(3)
     stats[2].start()
     for copy in stats:
         copy.wait_recv()
@@ -228,10 +255,14 @@
     out[...] = rows_of((target - log_total, log_total - tilted / total), (3, 8, third))
 
     w_send.wait_send()
-    for k in range(6):
+
+    def sent(k, carry):
         X(k).wait_send()
         Y(k).wait_send()
         Z(k).wait_send()
+        return carry
+
+    lax.fori_loop(0, waves, sent, 0)
     for copy in goals + stats:
         copy.wait_send()
     for k in range(1, nz):
@@ -256,11 +287,12 @@
             pltpu.VMEM((2 * entries, width), jnp.bfloat16),
             pltpu.VMEM((3, third, width), jnp.float32),
             pltpu.VMEM((4, 3, 8, third), jnp.int32),
+            pltpu.VMEM((4, 3, 4, 8, third), jnp.float32),
             pltpu.VMEM((4, 3, 8, third), jnp.float32),
             pltpu.VMEM((4, 3, 8, third), jnp.float32),
             pltpu.VMEM((nz, 3, 8, third), jnp.float32),
             dma((3,)), dma((3,)),
-            dma((6,)), dma((6,)), dma((6,)), dma((6,)), dma((6,)), dma((6,)),
+            *[dma((3 * PIECES,)) for _ in range(6)],
             dma((3,)), dma((3,)), dma((3,)), dma((3,)),
             dma((nz - 1,)), dma((nz - 1,)),
         ],

time: 107 us -> 104 us (0.972)
  Pallas kernels: 102 us -> 99.2 us
    pallas_call x1, Pallas kernels: 102 us -> 99.2 us  [fused(): pl.pallas_call(functools.partial(kernel, nz), out_shape=jax.ShapeDtypeStr...]
where the time goes in v2:
time: 104 us; the launch traced here: 103 us
  Pallas kernels  99.2 us (95%)
  local copies, waits for them, and re-layouts  2.15 us (2%)
  between operations  1.29 us (1%)
    pallas_call x1, Pallas kernels, fused(): pl.pallas_call(functools.partial(kernel, nz), out_shape=jax.ShapeDtypeStr...  99.2 us

profile of v2, /device:TPU:0, one launch (start us, length us, event | category | flops | bytes accessed | tf_op | source)
XLA Modules:
  0.0 103.3 jit_solution(15358988783079419113)
XLA Ops:
  0.6 0.7 broadcast_in_dim.12
  1.3 0.6 broadcast_in_dim.13.goal
  1.9 99.2 %shard_map.68 = f32[3,8,256]{2,1,0:T(8,128)} custom-call(f32[768,2048]{1,0:T(8,128)} %hid.1, f32[1,2048]{1,0:T(1,128)} %bitcast.3, bf16[1024,2048]{1,0:T(8,128)(2,1)} %head.1, s32[3,8,256]{2,1,0:T(8,128)} %broadcast_in_dim.13.goal), custom_call_target="tpu_custom_call" | custom-call | flops 25769803776 | bytes 10485760 | tf_op jit(solution)/shard_map/pallas_call | solution.py:280
  101.2 0.8 slice_reduce_fusion
  102.7 0.6 fusion
  (2 shorter events, 0.0 us)

commit v3 on v1

--- a/solution.py
+++ b/solution.py
@@ -11,6 +11,8 @@
 lowest = -1e30
 MESH = pl.DeviceIdType.MESH
 BLOCK = 512
+PIECES = 4
+WINDOW = 2
 
 
 def merge(parts):
@@ -54,8 +56,9 @@
     far_z = [(dp, lax.rem(z + k, nz)) for k in range(1, nz)]
     partners = [near_core, near_x, near_y, near_d] + far_z
 
-    third = T.shape[2]
-    half = third // 2
+    width, third = T.shape[2:]
+    size = width // PIECES
+    waves = 3 * PIECES
     entries = head.shape[0]
     base = (z * lax.axis_size("dp") + dp - core) * entries
 
@@ -71,26 +74,26 @@
         )
 
     def piece(slot, t, k):
-        return T.at[slot, t, pl.ds((k % 2) * half, half)]
+        return T.at[slot, t, pl.ds(lax.rem(k, PIECES) * size, size)]
 
     def X(k):
-        if k < 4:
-            t = q if k < 2 else p
-            return send(piece(0, t, k), piece(1, t, k), xs.at[k], xr.at[k], near_x)
-        return send(piece(2, p, k), piece(3, p, k), xs.at[k], xr.at[k], near_x)
+        g = lax.div(k, PIECES)
+        d, t = lax.div(g, 2), q - lax.div(g + 1, 2)
+        return send(piece(2 * d, t, k), piece(1 + 2 * d, t, k), xs.at[k], xr.at[k], near_x)
 
     def Y(k):
-        if k < 4:
-            t = p if k < 2 else q
-            return send(piece(0, t, k), piece(2, t, k), ys.at[k], yr.at[k], near_y)
-        return send(piece(1, q, k), piece(3, q, k), ys.at[k], yr.at[k], near_y)
+        g = lax.div(k, PIECES)
+        d, t = lax.div(g, 2), p + lax.div(g + 1, 2)
+        return send(piece(d, t, k), piece(2 + d, t, k), ys.at[k], yr.at[k], near_y)
 
     def Z(k):
-        slot = (2 - p, 1 + p, 3)[k // 2]
+        g = lax.div(k, PIECES)
+        slot = jnp.where(g == 0, 2 - p, jnp.where(g == 1, 1 + p, 3))
         return send(piece(slot, s, k), piece(slot, s, k), zs.at[k], zr.at[k], near_z)
 
     def Z_in(k):
-        slot = (1 + p, 2 - p, 3)[k // 2]
+        g = lax.div(k, PIECES)
+        slot = jnp.where(g == 0, 1 + p, jnp.where(g == 1, 2 - p, 3))
         return send(piece(slot, m, k), piece(slot, m, k), zs.at[k], zr.at[k], near_z)
 
     own_rows = pl.ds(core * entries, entries)
@@ -118,30 +121,30 @@
         load(t).wait()
         states = raw[t]
         scale = lax.rsqrt(jnp.mean(states * states, axis=1, keepdims=True) + epsilon)
-        T[0, t] = (states * scale * gain[...]).astype(jnp.bfloat16)
+        T[0, t] = (states * scale * gain[...]).astype(jnp.bfloat16).T
 
     normalise(p)
     pl.semaphore_wait(barrier, len(partners))
-    Y(0).start()
+    for k in range(WINDOW):
+        Y(k).start()
     w_send.start()
-    Y(1).start()
     normalise(q)
-    X(0).start()
-    X(1).start()
+    for k in range(WINDOW):
+        X(k).start()
     for copy in goals:
         copy.start()
     normalise(m)
     tgt[0] = goal[...]
+    w_local.wait()
+    w_in.wait_recv()
 
     def unit(slot, t):
         wanted = tgt[slot, t, 0:1, :] - base
-
-        def body(i, carry):
-            top, total, tilted, target = carry
-            rows = pl.ds(pl.multiple_of(i * BLOCK, BLOCK), BLOCK)
-            logits = lax.dot_general(
-                W[rows, :], T[slot, t], (((1,), (1,)), ((), ())),
-                preferred_element_type=jnp.float32,
+        zero = jnp.zeros((8, third), jnp.float32)
+        top, total, tilted, target = jnp.full((8, third), lowest, jnp.float32), zero, zero, zero
+        for i in range(W.shape[0] // BLOCK):
+            logits = jnp.dot(
+                W[pl.ds(i * BLOCK, BLOCK), :], T[slot, t], preferred_element_type=jnp.float32
             )
             entry = lax.broadcasted_iota(jnp.int32, logits.shape, 0)
             hit = jnp.where(entry == wanted - i * BLOCK, logits, 0.0)
@@ -152,12 +155,7 @@
             weights = jnp.exp(logits - higher[None])
             total = total * factor + jnp.sum(weights, axis=0)
             tilted = tilted * factor + jnp.sum(weights * logits, axis=0)
-            return higher, total, tilted, target
-
-        zero = jnp.zeros((8, third), jnp.float32)
-        top, total, tilted, target = lax.fori_loop(
-            0, W.shape[0] // BLOCK, body, (jnp.full((8, third), lowest, jnp.float32), zero, zero, zero)
-        )
+            top = higher
         highest = jnp.max(top, axis=0, keepdims=True)
         factor = jnp.exp(top - highest)
         st[slot, t] = rows_of(
@@ -170,46 +168,51 @@
             (8, third),
         )
 
-    def wave(k):
-        X(k).wait_recv()
-        Y(k).wait_recv()
-        if k < 4:
-            X(k + 2).start()
-            Y(k + 2).start()
-        Z(k).start()
-
-    def units(count, pick):
-        def step(u, carry):
-            unit(*pick(u))
-            return carry
-
-        lax.fori_loop(0, count, step, 0)
-
-    w_local.wait()
-    w_in.wait_recv()
-    units(2, lambda u: (0, p + u))
-    wave(0)
-    units(1, lambda u: (0, m))
-    for copy in goals:
-        copy.wait_recv()
-    wave(1)
-    units(2, lambda u: (1 + u, q - u))
-    wave(2)
-    Z_in(0).wait_recv()
-    Z_in(1).wait_recv()
-    wave(3)
-    units(3, lambda u: (jnp.where(u == 2, 1 + p, 1 + u), jnp.where(u == 2, m, p + u)))
-    wave(4)
-    Z_in(2).wait_recv()
-    Z_in(3).wait_recv()
-    units(1, lambda u: (2 - p, m))
-    stats[0].start()
-    stats[1].start()
-    wave(5)
-    units(2, lambda u: (3, p + u))
-    Z_in(4).wait_recv()
-    Z_in(5).wait_recv()
-    units(1, lambda u: (3, m))
+    def pick(g, u):
+        slot = jnp.where(g == 0, 0, jnp.where(g == 3, 3, 1 + u))
+        t = jnp.where(g == 1, q - u, p + u)
+        late = jnp.where(g == 1, 1 + p, jnp.where(g == 2, 2 - p, g))
+        return jnp.where(u == 2, late, slot), jnp.where(u == 2, m, t)
+
+    def step(k, carry):
+        g, j = lax.div(k, PIECES), lax.rem(k, PIECES)
+
+        @pl.when(k < waves)
+        def _():
+            X(k).wait_recv()
+            Y(k).wait_recv()
+            Z(k).start()
+
+        @pl.when(k + WINDOW < waves)
+        def _():
+            X(k + WINDOW).start()
+            Y(k + WINDOW).start()
+
+        @pl.when(k == PIECES)
+        def _():
+            for copy in goals:
+                copy.wait_recv()
+
+        @pl.when(k == waves)
+        def _():
+            stats[0].start()
+            stats[1].start()
+
+        @pl.when((j == 2) & (g > 0))
+        def _():
+            def arrive(i, carry):
+                Z_in((g - 1) * PIECES + i).wait_recv()
+                return carry
+
+            lax.fori_loop(0, PIECES, arrive, 0)
+
+        @pl.when(j < 3)
+        def _():
+            unit(*pick(g, j))
+
+        return carry
+
+    lax.fori_loop(0, waves + 3, step, 0)
     stats[2].start()
     for copy in stats:
         copy.wait_recv()
@@ -228,10 +231,14 @@
     out[...] = rows_of((target - log_total, log_total - tilted / total), (3, 8, third))
 
     w_send.wait_send()
-    for k in range(6):
+
+    def sent(k, carry):
         X(k).wait_send()
         Y(k).wait_send()
         Z(k).wait_send()
+        return carry
+
+    lax.fori_loop(0, waves, sent, 0)
     for copy in goals + stats:
         copy.wait_send()
     for k in range(1, nz):
@@ -252,7 +259,7 @@
         in_specs=[any_space, vmem, any_space, vmem],
         out_specs=vmem,
         scratch_shapes=[
-            pltpu.VMEM((4, 3, third, width), jnp.bfloat16),
+            pltpu.VMEM((4, 3, width, third), jnp.bfloat16),
             pltpu.VMEM((2 * entries, width), jnp.bfloat16),
             pltpu.VMEM((3, third, width), jnp.float32),
             pltpu.VMEM((4, 3, 8, third), jnp.int32),
@@ -260,7 +267,7 @@
             pltpu.VMEM((4, 3, 8, third), jnp.float32),
             pltpu.VMEM((nz, 3, 8, third), jnp.float32),
             dma((3,)), dma((3,)),
-            dma((6,)), dma((6,)), dma((6,)), dma((6,)), dma((6,)), dma((6,)),
+            *[dma((3 * PIECES,)) for _ in range(6)],
             dma((3,)), dma((3,)), dma((3,)), dma((3,)),
             dma((nz - 1,)), dma((nz - 1,)),
         ],

time: 107 us -> 99.9 us (0.934)
  Pallas kernels: 102 us -> 95.5 us
    pallas_call x1, Pallas kernels: 102 us -> 95.5 us  [fused(): pl.pallas_call(functools.partial(kernel, nz), out_shape=jax.ShapeDtypeStr...]
where the time goes in v3:
time: 99.9 us; the launch traced here: 99.6 us
  Pallas kernels  95.5 us (96%)
  local copies, waits for them, and re-layouts  2.15 us (2%)
  between operations  1.29 us (1%)
    pallas_call x1, Pallas kernels, fused(): pl.pallas_call(functools.partial(kernel, nz), out_shape=jax.ShapeDtypeStr...  95.5 us

profile of v3, /device:TPU:0, one launch (start us, length us, event | category | flops | bytes accessed | tf_op | source)
XLA Modules:
  0.0 99.6 jit_solution(10440645170387413958)
XLA Ops:
  0.6 0.7 broadcast_in_dim.12
  1.3 0.6 broadcast_in_dim.13.goal
  1.9 95.5 %shard_map.68 = f32[3,8,256]{2,1,0:T(8,128)} custom-call(f32[768,2048]{1,0:T(8,128)} %hid.1, f32[1,2048]{1,0:T(1,128)} %bitcast.3, bf16[1024,2048]{1,0:T(8,128)(2,1)} %head.1, s32[3,8,256]{2,1,0:T(8,128)} %broadcast_in_dim.13.goal), custom_call_target="tpu_custom_call" | custom-call | flops 25769803776 | bytes 10485760 | tf_op jit(solution)/shard_map/pallas_call | solution.py:256
  97.5 0.8 slice_reduce_fusion
  99.0 0.6 fusion
  (2 shorter events, 0.0 us)

commit v4 on v3

--- a/solution.py
+++ b/solution.py
@@ -11,8 +11,10 @@
 lowest = -1e30
 MESH = pl.DeviceIdType.MESH
 BLOCK = 512
-PIECES = 4
-WINDOW = 2
+PIECES = 8
+WINDOW = 5
+FIRST = 3
+STRIDE = 2
 
 
 def merge(parts):
@@ -37,7 +39,7 @@
     return tile
 
 
-def kernel(nz, hid, gain, head, goal, out, T, W, raw, tgt, st, rs, rz,
+def kernel(nz, hid, gain, head, ids, lengths, log_probs, entropies, T, W, raw, goal, tgt, st, rs, rz,
            hid_sem, w_sem, xs, xr, ys, yr, zs, zr, gs, gr, ss, sr, vs, vr):
     dp = lax.axis_index("dp")
     z = lax.axis_index("vocab")
@@ -62,6 +64,9 @@
     entries = head.shape[0]
     base = (z * lax.axis_size("dp") + dp - core) * entries
 
+    for t in range(3):
+        goal[t] = jnp.broadcast_to(ids[pl.ds(t * third, third)][None, :], (8, third))
+
     def load(t):
         return pltpu.make_async_copy(
             hid.at[pl.ds(t * third, third)], raw.at[t], hid_sem.at[t]
@@ -121,7 +126,7 @@
         load(t).wait()
         states = raw[t]
         scale = lax.rsqrt(jnp.mean(states * states, axis=1, keepdims=True) + epsilon)
-        T[0, t] = (states * scale * gain[...]).astype(jnp.bfloat16).T
+        T[0, t] = (states * scale * gain[...][None, :]).astype(jnp.bfloat16).T
 
     normalise(p)
     pl.semaphore_wait(barrier, len(partners))
@@ -135,8 +140,6 @@
         copy.start()
     normalise(m)
     tgt[0] = goal[...]
-    w_local.wait()
-    w_in.wait_recv()
 
     def unit(slot, t):
         wanted = tgt[slot, t, 0:1, :] - base
@@ -176,20 +179,34 @@
 
     def step(k, carry):
         g, j = lax.div(k, PIECES), lax.rem(k, PIECES)
+        tail = k >= waves
+        u = jnp.where(tail, j, lax.div(j - FIRST, STRIDE))
+        turn = tail | ((j >= FIRST) & (lax.rem(j - FIRST + PIECES * STRIDE, STRIDE) == 0))
 
         @pl.when(k < waves)
         def _():
             X(k).wait_recv()
+
+        @pl.when(k + WINDOW < waves)
+        def _():
+            X(k + WINDOW).start()
+
+        @pl.when(k < waves)
+        def _():
             Y(k).wait_recv()
+
+        @pl.when(k + WINDOW < waves)
+        def _():
+            Y(k + WINDOW).start()
+
+        @pl.when(k < waves)
+        def _():
             Z(k).start()
 
-        @pl.when(k + WINDOW < waves)
-        def _():
-            X(k + WINDOW).start()
-            Y(k + WINDOW).start()
-
-        @pl.when(k == PIECES)
-        def _():
+        @pl.when(k == FIRST)
+        def _():
+            w_local.wait()
+            w_in.wait_recv()
             for copy in goals:
                 copy.wait_recv()
 
@@ -198,7 +215,7 @@
             stats[0].start()
             stats[1].start()
 
-        @pl.when((j == 2) & (g > 0))
+        @pl.when(turn & (u == 2) & (g > 0))
         def _():
             def arrive(i, carry):
                 Z_in((g - 1) * PIECES + i).wait_recv()
@@ -206,9 +223,9 @@
 
             lax.fori_loop(0, PIECES, arrive, 0)
 
-        @pl.when(j < 3)
-        def _():
-            unit(*pick(g, j))
+        @pl.when(turn)
+        def _():
+            unit(*pick(g, u))
 
         return carry
 
@@ -228,7 +245,14 @@
         V(k, lax.rem(z + nz - k, nz)).wait_recv()
     top, total, tilted, target = merge([rz[i] for i in range(nz)])
     log_total = top + jnp.log(total)
-    out[...] = rows_of((target - log_total, log_total - tilted / total), (3, 8, third))
+    chosen = target - log_total
+    spread = log_total - tilted / total
+    for t in range(3):
+        slots = pl.ds(t * third, third)
+        position = lax.broadcasted_iota(jnp.int32, (1, third), 1) + t * third
+        live = position < lengths[0]
+        log_probs[slots] = jnp.where(live, chosen[t], 0.0)[0]
+        entropies[slots] = jnp.where(live, spread[t], 0.0)[0]
 
     w_send.wait_send()
 
@@ -249,19 +273,19 @@
     rows, width = hidden_states.shape
     entries = head_weight.shape[0]
     third = rows // 3
-    goal = jnp.broadcast_to(target_ids.reshape(3, 1, third), (3, 8, third))
     dma = pltpu.SemaphoreType.DMA
     any_space = pl.BlockSpec(memory_space=pl.ANY)
     vmem = pl.BlockSpec(memory_space=pltpu.VMEM)
-    scores = pl.pallas_call(
+    return pl.pallas_call(
         functools.partial(kernel, nz),
-        out_shape=jax.ShapeDtypeStruct((3, 8, third), jnp.float32),
-        in_specs=[any_space, vmem, any_space, vmem],
-        out_specs=vmem,
+        out_shape=(jax.ShapeDtypeStruct((rows,), jnp.float32),) * 2,
+        in_specs=[any_space, vmem, any_space, vmem, pl.BlockSpec(memory_space=pltpu.SMEM)],
+        out_specs=(vmem, vmem),
         scratch_shapes=[
             pltpu.VMEM((4, 3, width, third), jnp.bfloat16),
             pltpu.VMEM((2 * entries, width), jnp.bfloat16),
             pltpu.VMEM((3, third, width), jnp.float32),
+            pltpu.VMEM((3, 8, third), jnp.int32),
             pltpu.VMEM((4, 3, 8, third), jnp.int32),
             pltpu.VMEM((4, 3, 8, third), jnp.float32),
             pltpu.VMEM((4, 3, 8, third), jnp.float32),
@@ -279,11 +303,7 @@
             bytes_accessed=rows * width * 4 + entries * width * 2,
             transcendentals=4 * rows * 2 * entries,
         ),
-    )(hidden_states, norm_gain.reshape(1, width), head_weight, goal)
-    live = jnp.arange(rows, dtype=jnp.int32) < lengths[0]
-    log_probs = jnp.where(live, scores[:, 0, :].reshape(rows), 0.0)
-    entropies = jnp.where(live, scores[:, 1, :].reshape(rows), 0.0)
-    return (log_probs, entropies)
+    )(hidden_states, norm_gain, head_weight, target_ids, lengths)
 
 
 def gathered(hidden_states, norm_gain, head_weight, target_ids, lengths):

time: 99.9 us -> 103 us (1.031)
  Pallas kernels: 95.5 us -> 98.5 us
    pallas_call x1, Pallas kernels: 95.5 us -> 98.5 us  [fused(): pl.pallas_call(functools.partial(kernel, nz), out_shape=(jax.ShapeDtypeSt...]
    unnamed x0 -> x2, local copies, waits for them, and re-layouts: none -> 2.53 us
    broadcast_in_dim x2 -> x0, local copies, waits for them, and re-layouts: 1.29 us -> none  [fused(): goal = jnp.broadcast_to(target_ids.reshape(3, 1, third), (3, 8, third))]
where the time goes in v4:
time: 103 us; the launch traced here: 102 us
  Pallas kernels  98.5 us (96%)
  local copies, waits for them, and re-layouts  2.53 us (2%)
  between operations  1.29 us (1%)
    pallas_call x1, Pallas kernels, fused(): pl.pallas_call(functools.partial(kernel, nz), out_shape=(jax.ShapeDtypeSt...  98.5 us
    unnamed x2, local copies, waits for them, and re-layouts  2.53 us

profile of v4, /device:TPU:0, one launch (start us, length us, event | category | flops | bytes accessed | tf_op | source)
XLA Modules:
  0.0 102.3 jit_solution(10842725772280757463)
XLA Ops:
  1.3 98.5 %shard_map.68 = (f32[768]{0:T(1024)}, f32[768]{0:T(1024)}) custom-call(f32[768,2048]{1,0:T(8,128)} %hid.1, f32[2048]{0:T(1024)} %gain.1, bf16[1024,2048]{1,0:T(8,128)(2,1)} %head.1, s32[768]{0:T(1024)} %ids.1, s32[1]{0:T(128)S(6)} %copy.9.lengths), custom_call_target="tpu_custom_call" | custom-call | flops 25769803776 | bytes 10485760 | tf_op jit(solution)/shard_map/pallas_call | solution.py:279
  99.8 1.3 %copy.10 = f32[768]{0:T(1024)} copy(f32[768]{0:T(1024)} %get-tuple-element.4) | data formatting | bytes 6144
  101.0 1.3 %copy.11 = f32[768]{0:T(1024)} copy(f32[768]{0:T(1024)} %get-tuple-element.5) | data formatting | bytes 6144

commit v5 on v4

--- a/solution.py
+++ b/solution.py
@@ -10,10 +10,10 @@
 epsilon = 1e-05
 lowest = -1e30
 MESH = pl.DeviceIdType.MESH
-BLOCK = 512
+BLOCK = 1024
 PIECES = 8
-WINDOW = 5
-FIRST = 3
+WINDOW = 3
+FIRST = 1
 STRIDE = 2
 
 
@@ -181,7 +181,7 @@
         g, j = lax.div(k, PIECES), lax.rem(k, PIECES)
         tail = k >= waves
         u = jnp.where(tail, j, lax.div(j - FIRST, STRIDE))
-        turn = tail | ((j >= FIRST) & (lax.rem(j - FIRST + PIECES * STRIDE, STRIDE) == 0))
+        turn = tail | ((j >= FIRST) & (u < 3) & (lax.rem(j - FIRST + PIECES * STRIDE, STRIDE) == 0))
 
         @pl.when(k < waves)
         def _():

time: 103 us -> 100 us (0.971)
  Pallas kernels: 98.5 us -> 96 us
    pallas_call x1, Pallas kernels: 98.5 us -> 96 us  [fused(): pl.pallas_call(functools.partial(kernel, nz), out_shape=(jax.ShapeDtypeSt...]
where the time goes in v5:
time: 100 us; the launch traced here: 99.8 us
  Pallas kernels  96 us (96%)
  local copies, waits for them, and re-layouts  2.53 us (3%)
  between operations  1.29 us (1%)
    pallas_call x1, Pallas kernels, fused(): pl.pallas_call(functools.partial(kernel, nz), out_shape=(jax.ShapeDtypeSt...  96 us
    unnamed x2, local copies, waits for them, and re-layouts  2.53 us

profile of v5, /device:TPU:0, one launch (start us, length us, event | category | flops | bytes accessed | tf_op | source)
XLA Modules:
  0.0 99.8 jit_solution(6238092985723580546)
XLA Ops:
  1.3 96.0 %shard_map.68 = (f32[768]{0:T(1024)}, f32[768]{0:T(1024)}) custom-call(f32[768,2048]{1,0:T(8,128)} %hid.1, f32[2048]{0:T(1024)} %gain.1, bf16[1024,2048]{1,0:T(8,128)(2,1)} %head.1, s32[768]{0:T(1024)} %ids.1, s32[1]{0:T(128)S(6)} %copy.9.lengths), custom_call_target="tpu_custom_call" | custom-call | flops 25769803776 | bytes 10485760 | tf_op jit(solution)/shard_map/pallas_call | solution.py:279
  97.3 1.3 %copy.10 = f32[768]{0:T(1024)} copy(f32[768]{0:T(1024)} %get-tuple-element.4) | data formatting | bytes 6144
  98.6 1.3 %copy.11 = f32[768]{0:T(1024)} copy(f32[768]{0:T(1024)} %get-tuple-element.5) | data formatting | bytes 6144

commit v6 on v5

--- a/solution.py
+++ b/solution.py
@@ -10,11 +10,11 @@
 epsilon = 1e-05
 lowest = -1e30
 MESH = pl.DeviceIdType.MESH
-BLOCK = 1024
-PIECES = 8
-WINDOW = 3
-FIRST = 1
-STRIDE = 2
+BLOCK = 256
+PIECES = 4
+WINDOW = 2
+FIRST = 0
+STRIDE = 1
 
 
 def merge(parts):
@@ -130,25 +130,33 @@
 
     normalise(p)
     pl.semaphore_wait(barrier, len(partners))
-    for k in range(WINDOW):
-        Y(k).start()
+    Y(0).start()
     w_send.start()
     normalise(q)
-    for k in range(WINDOW):
-        X(k).start()
+    X(0).start()
     for copy in goals:
         copy.start()
     normalise(m)
     tgt[0] = goal[...]
+    for k in range(1, WINDOW):
+        Y(k).start()
+        X(k).start()
 
     def unit(slot, t):
         wanted = tgt[slot, t, 0:1, :] - base
         zero = jnp.zeros((8, third), jnp.float32)
         top, total, tilted, target = jnp.full((8, third), lowest, jnp.float32), zero, zero, zero
-        for i in range(W.shape[0] // BLOCK):
-            logits = jnp.dot(
+        def score(i):
+            return jnp.dot(
                 W[pl.ds(i * BLOCK, BLOCK), :], T[slot, t], preferred_element_type=jnp.float32
             )
+
+        blocks = W.shape[0] // BLOCK
+        following = score(0)
+        for i in range(blocks):
+            logits = following
+            if i + 1 < blocks:
+                following = score(i + 1)
             entry = lax.broadcasted_iota(jnp.int32, logits.shape, 0)
             hit = jnp.where(entry == wanted - i * BLOCK, logits, 0.0)
             target = target + jnp.sum(hit.reshape(BLOCK // 8, 8, third), axis=0)

time: 100 us -> 99.6 us (level)
  no operation moved by 1% of the time
where the time goes in v6:
time: 99.6 us; the launch traced here: 99.4 us
  Pallas kernels  95.5 us (96%)
  local copies, waits for them, and re-layouts  2.53 us (3%)
  between operations  1.29 us (1%)
    pallas_call x1, Pallas kernels, fused(): pl.pallas_call(functools.partial(kernel, nz), out_shape=(jax.ShapeDtypeSt...  95.5 us
    unnamed x2, local copies, waits for them, and re-layouts  2.53 us

profile of v6, /device:TPU:0, one launch (start us, length us, event | category | flops | bytes accessed | tf_op | source)
XLA Modules:
  0.0 99.4 jit_solution(3459186898962171481)
XLA Ops:
  1.3 95.5 %shard_map.68 = (f32[768]{0:T(1024)}, f32[768]{0:T(1024)}) custom-call(f32[768,2048]{1,0:T(8,128)} %hid.1, f32[2048]{0:T(1024)} %gain.1, bf16[1024,2048]{1,0:T(8,128)(2,1)} %head.1, s32[768]{0:T(1024)} %ids.1, s32[1]{0:T(128)S(6)} %copy.9.lengths), custom_call_target="tpu_custom_call" | custom-call | flops 25769803776 | bytes 10485760 | tf_op jit(solution)/shard_map/pallas_call | solution.py:287
  96.8 1.3 %copy.10 = f32[768]{0:T(1024)} copy(f32[768]{0:T(1024)} %get-tuple-element.4) | data formatting | bytes 6144
  98.1 1.3 %copy.11 = f32[768]{0:T(1024)} copy(f32[768]{0:T(1024)} %get-tuple-element.5) | data formatting | bytes 6144

commit v7 on v6

--- a/solution.py
+++ b/solution.py
@@ -13,8 +13,6 @@
 BLOCK = 256
 PIECES = 4
 WINDOW = 2
-FIRST = 0
-STRIDE = 1
 
 
 def merge(parts):
@@ -39,7 +37,7 @@
     return tile
 
 
-def kernel(nz, hid, gain, head, ids, lengths, log_probs, entropies, T, W, raw, goal, tgt, st, rs, rz,
+def kernel(nz, hid, gain, head, ids, lengths, log_probs, entropies, T, W, raw, begun, goal, tgt, st, rs, rz,
            hid_sem, w_sem, xs, xr, ys, yr, zs, zr, gs, gr, ss, sr, vs, vr):
     dp = lax.axis_index("dp")
     z = lax.axis_index("vocab")
@@ -122,36 +120,63 @@
         pl.semaphore_signal(barrier, inc=1, device_id=where, device_id_type=MESH)
     w_local.start()
 
-    def normalise(t):
+    def scale_of(t):
         load(t).wait()
         states = raw[t]
-        scale = lax.rsqrt(jnp.mean(states * states, axis=1, keepdims=True) + epsilon)
-        T[0, t] = (states * scale * gain[...][None, :]).astype(jnp.bfloat16).T
-
-    normalise(p)
+        return lax.rsqrt(jnp.mean(states * states, axis=1, keepdims=True) + epsilon)
+
+    def normalise(t, scale, j):
+        part = pl.ds(j * size, size)
+        T[0, t, part, :] = (raw[t, :, part] * scale * gain[part][None, :]).astype(jnp.bfloat16).T
+
+    scale_p = scale_of(p)
+    normalise(p, scale_p, 0)
     pl.semaphore_wait(barrier, len(partners))
     Y(0).start()
     w_send.start()
-    normalise(q)
+    scale_q = scale_of(q)
+    normalise(q, scale_q, 0)
     X(0).start()
+    for k in range(1, WINDOW):
+        normalise(p, scale_p, k)
+        Y(k).start()
+        normalise(q, scale_q, k)
+        X(k).start()
     for copy in goals:
         copy.start()
-    normalise(m)
+    for k in range(WINDOW, PIECES):
+        normalise(p, scale_p, k)
+        normalise(q, scale_q, k)
+    scale_m = scale_of(m)
+    for k in range(PIECES):
+        normalise(m, scale_m, k)
     tgt[0] = goal[...]
-    for k in range(1, WINDOW):
-        Y(k).start()
-        X(k).start()
-
-    def unit(slot, t):
+
+    middle = width // 2
+    blocks = W.shape[0] // BLOCK
+
+    def begin(u, t):
+        for i in range(blocks):
+            rows = pl.ds(i * BLOCK, BLOCK)
+            begun[u, rows, :] = jnp.dot(
+                W[rows, pl.ds(0, middle)], T[3, t, pl.ds(0, middle), :],
+                preferred_element_type=jnp.float32,
+            )
+
+    def end(u, t):
+        def score(i):
+            rows = pl.ds(i * BLOCK, BLOCK)
+            return begun[u, rows, :] + jnp.dot(
+                W[rows, pl.ds(middle, middle)], T[3, t, pl.ds(middle, middle), :],
+                preferred_element_type=jnp.float32,
+            )
+
+        unit(3, t, score)
+
+    def unit(slot, t, score):
         wanted = tgt[slot, t, 0:1, :] - base
         zero = jnp.zeros((8, third), jnp.float32)
         top, total, tilted, target = jnp.full((8, third), lowest, jnp.float32), zero, zero, zero
-        def score(i):
-            return jnp.dot(
-                W[pl.ds(i * BLOCK, BLOCK), :], T[slot, t], preferred_element_type=jnp.float32
-            )
-
-        blocks = W.shape[0] // BLOCK
         following = score(0)
         for i in range(blocks):
             logits = following
@@ -179,65 +204,78 @@
             (8, third),
         )
 
+    def whole(slot, t):
+        def score(i):
+            return jnp.dot(
+                W[pl.ds(i * BLOCK, BLOCK), :], T[slot, t], preferred_element_type=jnp.float32
+            )
+
+        unit(slot, t, score)
+
     def pick(g, u):
-        slot = jnp.where(g == 0, 0, jnp.where(g == 3, 3, 1 + u))
+        slot = jnp.where(g == 0, 0, 1 + u)
         t = jnp.where(g == 1, q - u, p + u)
-        late = jnp.where(g == 1, 1 + p, jnp.where(g == 2, 2 - p, g))
+        late = jnp.where(g == 1, 1 + p, jnp.where(g == 2, 2 - p, 0))
         return jnp.where(u == 2, late, slot), jnp.where(u == 2, m, t)
 
-    def step(k, carry):
-        g, j = lax.div(k, PIECES), lax.rem(k, PIECES)
-        tail = k >= waves
-        u = jnp.where(tail, j, lax.div(j - FIRST, STRIDE))
-        turn = tail | ((j >= FIRST) & (u < 3) & (lax.rem(j - FIRST + PIECES * STRIDE, STRIDE) == 0))
-
-        @pl.when(k < waves)
-        def _():
-            X(k).wait_recv()
+    def arrive(first, last):
+        def step(k, carry):
+            Z_in(k).wait_recv()
+            return carry
+
+        lax.fori_loop(first, last, step, 0)
+
+    def wave(k, carry):
+        g, u = lax.div(k, PIECES), lax.rem(k, PIECES)
+        X(k).wait_recv()
 
         @pl.when(k + WINDOW < waves)
         def _():
             X(k + WINDOW).start()
 
-        @pl.when(k < waves)
-        def _():
-            Y(k).wait_recv()
+        Y(k).wait_recv()
 
         @pl.when(k + WINDOW < waves)
         def _():
             Y(k + WINDOW).start()
 
-        @pl.when(k < waves)
-        def _():
-            Z(k).start()
-
-        @pl.when(k == FIRST)
+        Z(k).start()
+
+        @pl.when(k == 0)
         def _():
             w_local.wait()
             w_in.wait_recv()
             for copy in goals:
                 copy.wait_recv()
 
-        @pl.when(k == waves)
+        @pl.when((u == 2) & (g > 0))
         def _():
-            stats[0].start()
-            stats[1].start()
-
-        @pl.when(turn & (u == 2) & (g > 0))
+            arrive((g - 1) * PIECES, g * PIECES)
+
+        @pl.when(u < 3)
         def _():
-            def arrive(i, carry):
-                Z_in((g - 1) * PIECES + i).wait_recv()
-                return carry
-
-            lax.fori_loop(0, PIECES, arrive, 0)
-
-        @pl.when(turn)
-        def _():
-            unit(*pick(g, u))
+            whole(*pick(g, u))
 
         return carry
 
-    lax.fori_loop(0, waves + 3, step, 0)
+    def first_halves(u, carry):
+        begin(u, p + u)
+        return carry
+
+    def second_halves(u, carry):
+        end(u, p + u)
+        return carry
+
+    lax.fori_loop(0, waves - 1, wave, 0)
+    lax.fori_loop(0, 2, first_halves, 0)
+    wave(waves - 1, 0)
+    stats[0].start()
+    stats[1].start()
+    lax.fori_loop(0, 2, second_halves, 0)
+    arrive(2 * PIECES, 2 * PIECES + PIECES // 2)
+    begin(2, m)
+    arrive(2 * PIECES + PIECES // 2, waves)
+    end(2, m)
     stats[2].start()
     for copy in stats:
         copy.wait_recv()
@@ -293,6 +331,7 @@
             pltpu.VMEM((4, 3, width, third), jnp.bfloat16),
             pltpu.VMEM((2 * entries, width), jnp.bfloat16),
             pltpu.VMEM((3, third, width), jnp.float32),
+            pltpu.VMEM((3, 2 * entries, third), jnp.float32),
             pltpu.VMEM((3, 8, third), jnp.int32),
             pltpu.VMEM((4, 3, 8, third), jnp.int32),
             pltpu.VMEM((4, 3, 8, third), jnp.float32),

time: 99.6 us -> 101 us (1.014)
  Pallas kernels: 95.5 us -> 96.8 us
    pallas_call x1, Pallas kernels: 95.5 us -> 96.8 us  [fused(): pl.pallas_call(functools.partial(kernel, nz), out_shape=(jax.ShapeDtypeSt...]
where the time goes in v7:
time: 101 us
  Pallas kernels  96.8 us (96%)
  local copies, waits for them, and re-layouts  2.53 us (3%)
  between operations  1.29 us (1%)
    pallas_call x1, Pallas kernels, fused(): pl.pallas_call(functools.partial(kernel, nz), out_shape=(jax.ShapeDtypeSt...  96.8 us
    unnamed x2, local copies, waits for them, and re-layouts  2.53 us

profile of v7, /device:TPU:0, one launch (start us, length us, event | category | flops | bytes accessed | tf_op | source)
XLA Modules:
  0.0 100.7 jit_solution(15020275625241398092)
XLA Ops:
  1.3 96.8 %shard_map.68 = (f32[768]{0:T(1024)}, f32[768]{0:T(1024)}) custom-call(f32[768,2048]{1,0:T(8,128)} %hid.1, f32[2048]{0:T(1024)} %gain.1, bf16[1024,2048]{1,0:T(8,128)(2,1)} %head.1, s32[768]{0:T(1024)} %ids.1, s32[1]{0:T(128)S(6)} %copy.9.lengths), custom_call_target="tpu_custom_call" | custom-call | flops 25769803776 | bytes 10485760 | tf_op jit(solution)/shard_map/pallas_call | solution.py:325
  98.1 1.3 %copy.10 = f32[768]{0:T(1024)} copy(f32[768]{0:T(1024)} %get-tuple-element.4) | data formatting | bytes 6144
  99.4 1.3 %copy.11 = f32[768]{0:T(1024)} copy(f32[768]{0:T(1024)} %get-tuple-element.5) | data formatting | bytes 6144

commit v8 on v6

--- a/solution.py
+++ b/solution.py
@@ -10,7 +10,7 @@
 epsilon = 1e-05
 lowest = -1e30
 MESH = pl.DeviceIdType.MESH
-BLOCK = 256
+BLOCK = 512
 PIECES = 4
 WINDOW = 2
 FIRST = 0
@@ -39,7 +39,7 @@
     return tile
 
 
-def kernel(nz, hid, gain, head, ids, lengths, log_probs, entropies, T, W, raw, goal, tgt, st, rs, rz,
+def kernel(nz, hid, gain, head, ids, lengths, log_probs, entropies, T, W, raw, scored, goal, tgt, st, rs, rz,
            hid_sem, w_sem, xs, xr, ys, yr, zs, zr, gs, gr, ss, sr, vs, vr):
     dp = lax.axis_index("dp")
     z = lax.axis_index("vocab")
@@ -143,30 +143,31 @@
         X(k).start()
 
     def unit(slot, t):
-        wanted = tgt[slot, t, 0:1, :] - base
+        ahead = tgt[slot, t] - base - lax.broadcasted_iota(jnp.int32, (8, third), 0)
         zero = jnp.zeros((8, third), jnp.float32)
         top, total, tilted, target = jnp.full((8, third), lowest, jnp.float32), zero, zero, zero
+
         def score(i):
-            return jnp.dot(
+            scored[i % 2] = jnp.dot(
                 W[pl.ds(i * BLOCK, BLOCK), :], T[slot, t], preferred_element_type=jnp.float32
             )
 
         blocks = W.shape[0] // BLOCK
-        following = score(0)
+        score(0)
         for i in range(blocks):
-            logits = following
             if i + 1 < blocks:
-                following = score(i + 1)
-            entry = lax.broadcasted_iota(jnp.int32, logits.shape, 0)
-            hit = jnp.where(entry == wanted - i * BLOCK, logits, 0.0)
-            target = target + jnp.sum(hit.reshape(BLOCK // 8, 8, third), axis=0)
-            logits = logits.reshape(BLOCK // 8, 8, third)
-            higher = jnp.maximum(top, jnp.max(logits, axis=0))
+                score(i + 1)
+            higher = top
+            for r in range(0, BLOCK, 8):
+                higher = jnp.maximum(higher, scored[i % 2, pl.ds(r, 8), :])
             factor = jnp.exp(top - higher)
-            weights = jnp.exp(logits - higher[None])
-            total = total * factor + jnp.sum(weights, axis=0)
-            tilted = tilted * factor + jnp.sum(weights * logits, axis=0)
-            top = higher
+            total, tilted, top = total * factor, tilted * factor, higher
+            for r in range(0, BLOCK, 8):
+                logits = scored[i % 2, pl.ds(r, 8), :]
+                weights = jnp.exp(logits - top)
+                total = total + weights
+                tilted = tilted + weights * logits
+                target = target + jnp.where(ahead == i * BLOCK + r, logits, 0.0)
         highest = jnp.max(top, axis=0, keepdims=True)
         factor = jnp.exp(top - highest)
         st[slot, t] = rows_of(
@@ -293,6 +294,7 @@
             pltpu.VMEM((4, 3, width, third), jnp.bfloat16),
             pltpu.VMEM((2 * entries, width), jnp.bfloat16),
             pltpu.VMEM((3, third, width), jnp.float32),
+            pltpu.VMEM((2, BLOCK, third), jnp.float32),
             pltpu.VMEM((3, 8, third), jnp.int32),
             pltpu.VMEM((4, 3, 8, third), jnp.int32),
             pltpu.VMEM((4, 3, 8, third), jnp.float32),

time: 99.6 us -> 99.6 us (level)
  no operation moved by 1% of the time
where the time goes in v8:
time: 99.6 us; the launch traced here: 99.3 us
  Pallas kernels  95.5 us (96%)
  local copies, waits for them, and re-layouts  2.53 us (3%)
  between operations  1.29 us (1%)
    pallas_call x1, Pallas kernels, fused(): pl.pallas_call(functools.partial(kernel, nz), out_shape=(jax.ShapeDtypeSt...  95.5 us
    unnamed x2, local copies, waits for them, and re-layouts  2.53 us

profile of v8, /device:TPU:0, one launch (start us, length us, event | category | flops | bytes accessed | tf_op | source)
XLA Modules:
  0.0 99.3 jit_solution(10994431714256973890)
XLA Ops:
  1.3 95.5 %shard_map.68 = (f32[768]{0:T(1024)}, f32[768]{0:T(1024)}) custom-call(f32[768,2048]{1,0:T(8,128)} %hid.1, f32[2048]{0:T(1024)} %gain.1, bf16[1024,2048]{1,0:T(8,128)(2,1)} %head.1, s32[768]{0:T(1024)} %ids.1, s32[1]{0:T(128)S(6)} %copy.9.lengths), custom_call_target="tpu_custom_call" | custom-call | flops 25769803776 | bytes 10485760 | tf_op jit(solution)/shard_map/pallas_call | solution.py:288
  96.8 1.3 %copy.10 = f32[768]{0:T(1024)} copy(f32[768]{0:T(1024)} %get-tuple-element.4) | data formatting | bytes 6144
  98.1 1.3 %copy.11 = f32[768]{0:T(1024)} copy(f32[768]{0:T(1024)} %get-tuple-element.5) | data formatting | bytes 6144

commit v9 on v8

--- a/solution.py
+++ b/solution.py
@@ -12,7 +12,7 @@
 MESH = pl.DeviceIdType.MESH
 BLOCK = 512
 PIECES = 4
-WINDOW = 2
+WINDOW = 3
 FIRST = 0
 STRIDE = 1
 

time: 99.6 us -> 99.6 us (level)
  no operation moved by 1% of the time
where the time goes in v9:
time: 99.6 us; the launch traced here: 99.3 us
  Pallas kernels  95.5 us (96%)
  local copies, waits for them, and re-layouts  2.53 us (3%)
  between operations  1.29 us (1%)
    pallas_call x1, Pallas kernels, fused(): pl.pallas_call(functools.partial(kernel, nz), out_shape=(jax.ShapeDtypeSt...  95.5 us
    unnamed x2, local copies, waits for them, and re-layouts  2.53 us

profile of v9, /device:TPU:0, one launch (start us, length us, event | category | flops | bytes accessed | tf_op | source)
XLA Modules:
  0.0 99.3 jit_solution(16834860939597972828)
XLA Ops:
  1.3 95.5 %shard_map.68 = (f32[768]{0:T(1024)}, f32[768]{0:T(1024)}) custom-call(f32[768,2048]{1,0:T(8,128)} %hid.1, f32[2048]{0:T(1024)} %gain.1, bf16[1024,2048]{1,0:T(8,128)(2,1)} %head.1, s32[768]{0:T(1024)} %ids.1, s32[1]{0:T(128)S(6)} %copy.9.lengths), custom_call_target="tpu_custom_call" | custom-call | flops 25769803776 | bytes 10485760 | tf_op jit(solution)/shard_map/pallas_call | solution.py:288
  96.8 1.3 %copy.10 = f32[768]{0:T(1024)} copy(f32[768]{0:T(1024)} %get-tuple-element.4) | data formatting | bytes 6144
  98.1 1.3 %copy.11 = f32[768]{0:T(1024)} copy(f32[768]{0:T(1024)} %get-tuple-element.5) | data formatting | bytes 6144
